TPU v7x, 32 devices: a whole 2x2x4 slice. The times are simulated.
32 devices in a mesh: grp: 4 (over x, core), wav: 8 (over z, y).
Axes of the slice: x: 2, y: 2, z: 4, core: 2. Of those that a mesh axis runs over, the one named last changes fastest.
Arguments:
- spectra: float32 [3, 8, 16, 2, 2560], P(None, 'grp', 'wav'), may hold values from -6 to 6
- legendre: float32 [16, 2560, 32], P('wav'), may hold values from -0.03125 to 0.03125
- wave_number: int32 [16], replicated, may hold values from 0 to 2559, as said below
- cycle_points: int32 [32], replicated, may hold values from 20 to 10256, as said below
- cycle_owner: int32 [64], replicated, may hold values from 0 to 63, each once
Outputs:
- grid_columns: float32 [64, 3, 8, 11264], P('grp', None, None, 'wav')
Inputs may be any that keep to these rules, and one draw needn't show every extreme that they name: `wave_number`: all distinct; entries 2 i and 2 i + 1 sum to 2559. `cycle_points`: each is 20 + 4 k for a whole k, rising with the latitude index; 20 and 10256 both occur. `cycle_owner`: A permutation of the cycles: 0 to 31 northern, 32 + i the southern mirror of latitude i.
All inputs are finite; a program needn't handle non-finite values.
Results may differ from a plain program's by a relative error of at most 0.0003.
Values sent between devices are 32-bit elements; how exact they have to be, the bound alone decides.
A program may use at most 128 MiB of HBM per device.

v0:
```python
import functools
import math

import jax
import jax.numpy as jnp
from jax import lax
from jax.experimental import pallas as pl
from jax.experimental.pallas import tpu as pltpu
from jax.sharding import PartitionSpec as P

RMAX = 10256
SLOTS = 8
VMEM_BYTES = 65000 * 2**10
MESH = pl.DeviceIdType.MESH


def iota(shape, dim):
    return lax.broadcasted_iota(jnp.int32, shape, dim)


def split(x):
    high = x.astype(jnp.bfloat16)
    return high, (x - high.astype(jnp.float32)).astype(jnp.bfloat16)


def dot(a, b, dims=((1,), (0,))):
    return lax.dot_general(a, b, (dims, ((), ())), preferred_element_type=jnp.float32)


def spread(groups, columns, spec_in, leg_in, wave, owner, out, spec, leg, rows, send, send_sem, recv_sem, in_sem):
    devices = groups * columns
    g, w = lax.axis_index("grp"), lax.axis_index("wav")
    barrier = pltpu.get_barrier_semaphore()
    loads = [
        pltpu.make_async_copy(spec_in, spec, in_sem.at[0]),
        pltpu.make_async_copy(leg_in, leg, in_sem.at[1]),
    ]
    for load in loads:
        load.start()

    def each(act):
        for over in range(groups):

            @pl.loop(1 if over == 0 else 0, columns, unroll=columns - (over == 0) if columns <= 8 else 1)
            def _(along):
                act(lax.rem(g + over, groups), lax.rem(w + along, columns))

    each(lambda *to: pl.semaphore_signal(barrier, inc=1, device_id=to, device_id_type=MESH))

    fields, levels, waves, _, degrees = spec.shape
    half = leg.shape[1]
    lanes = send.shape[2]
    lane_row = iota((1, groups * lanes), 1) // SLOTS
    cycle = jnp.zeros((1, groups * lanes), jnp.int32)
    for row in range(2 * half):
        cycle = jnp.where(lane_row == row, owner[row], cycle)
    northern = iota((half, groups * lanes), 0)
    pick = [
        (northern + h * half == cycle).astype(jnp.float32).astype(jnp.bfloat16) for h in range(2)
    ]
    slot = iota((16, groups * lanes), 1) % SLOTS == iota((16, groups * lanes), 0) // 2
    degree = iota((16, degrees), 1)
    placed = []
    for load in loads:
        load.wait()
    for q in range(waves):
        rows[q, 8:16, :] = jnp.zeros((8, degrees), jnp.float32)
        for f in range(fields):
            for l in range(levels):
                at = 2 * (f * levels + l)
                rows[q, at : at + 2, :] = spec[f, l, q]
        number = wave[w * waves + q]
        masked = jnp.where(degree + number < degrees, rows[q], 0.0)
        mirrored = jnp.where(degree % 2 == 0, masked, -masked)
        high, low = split(jnp.concatenate([masked, mirrored], axis=0))
        table_high, table_low = split(leg[q])
        both = dot(jnp.concatenate([high, low], axis=0), table_high, ((1,), (1,)))
        fourier = both[:32] + both[32:] + dot(high, table_low, ((1,), (1,)))
        total = jnp.zeros((16, groups * lanes), jnp.float32)
        for h in range(2):
            high, low = split(fourier[16 * h : 16 * h + 16])
            moved = dot(jnp.concatenate([high, low], axis=0), pick[h])
            total = total + moved[:16] + moved[16:]
        total = jnp.where(slot, total, 0.0)
        total = total[:8] + total[8:]
        total = total + pltpu.roll(total, 4, 0)
        placed.append(total + pltpu.roll(total, 2, 0))
    message = jnp.where(iota(placed[0].shape, 0) < 2, placed[0], placed[1])
    for to in range(groups):
        send[to] = message[:4, to * lanes : (to + 1) * lanes]
    out[g, w] = send[g]

    pl.semaphore_wait(barrier, devices - 1)

    def copy(to, source):
        return pltpu.make_async_remote_copy(
            src_ref=send.at[to[0]],
            dst_ref=out.at[source[0], source[1]],
            send_sem=send_sem.at[to[0], to[1]],
            recv_sem=recv_sem.at[source[0], source[1]],
            device_id=to,
            device_id_type=MESH,
        )

    each(lambda *to: copy(to, (g, w)).start())
    each(lambda *source: copy(source, source).wait_recv())
    each(lambda *to: copy(to, (g, w)).wait_send())


def reduced(x, length, inverse):
    turns = jnp.floor(x.astype(jnp.float32) * inverse).astype(jnp.int32)
    left = x - turns * length
    left = jnp.where(left < 0, left + length, left)
    return jnp.where(left >= length, left - length, left)


def cosine(x, length, inverse):
    left = reduced(x, length, inverse)
    left = jnp.where(2 * left > length, left - length, left)
    half = left.astype(jnp.float32) * (inverse * math.pi)
    square = half * half
    series = jnp.full_like(square, 1.0 / math.factorial(13))
    for power in (11, 9, 7, 5, 3, 1):
        sign = -1.0 if power % 4 == 3 else 1.0
        series = series * square + sign / math.factorial(power)
    sine = series * half
    return 1.0 - 2.0 * sine * sine


def synthesis(columns, got, wave, points, owner, out, coeffs, swapped, grid, out_sem):
    groups, lanes = got.shape[0], got.shape[3]
    depth = 4 * columns
    count, fields, level_total, segment = grid.shape
    levels = level_total // groups
    block = fields * level_total
    copies = -(-3 * depth // 128) * 128 // depth
    wide = copies * depth
    tiles = segment // 128
    tile_rows = -(-tiles // 8) * 8
    g, w = lax.axis_index("grp"), lax.axis_index("wav")

    x = jnp.concatenate([got[i].reshape(depth, lanes) for i in range(groups)], axis=1)
    even = iota(x.shape, 0) % 2 == 0
    partner = jnp.where(even, pltpu.roll(x, depth - 1, 0), pltpu.roll(x, 1, 0))
    target = iota((count * block, 1), 0)
    inner = lax.rem(target, block)
    level = lax.rem(inner, level_total)
    target = (
        lax.div(level, levels) * lanes
        + lax.div(target, block) * SLOTS
        + lax.div(inner, level_total) * levels
        + lax.rem(level, levels)
    )
    move = iota((count * block, groups * lanes), 1) == target
    move = move.astype(jnp.float32).astype(jnp.bfloat16)
    for values, ref in ((x, coeffs), (partner, swapped)):
        high, low = split(values)
        ref[...] = dot(move, jnp.concatenate([high] * copies, axis=0), ((1,), (1,))) + dot(
            move, jnp.concatenate([low] * copies, axis=0), ((1,), (1,))
        )

    deep = iota((depth, 128), 0)
    deep_wave = jnp.zeros((depth, 128), jnp.int32)
    across = iota((tile_rows, wide), 1) % depth
    across_wave = jnp.zeros((tile_rows, wide), jnp.int32)
    for q in range(depth // 2):
        deep_wave = jnp.where(deep // 2 == q, wave[q], deep_wave)
        across_wave = jnp.where(across // 2 == q, wave[q], across_wave)
    near = deep_wave * iota((depth, 128), 1)
    far = across_wave * (w * segment + 128 * iota((tile_rows, wide), 0))
    weight = jnp.where(across_wave == 0, 1.0, 2.0)
    rest = (iota((block * tiles, wide), 1) // depth) % 2 == 1
    point = iota((block, 128), 1) + w * segment

    def write(p):
        return pltpu.make_async_copy(grid.at[p], out.at[p], out_sem.at[p])

    @pl.loop(0, count, unroll=16)
    def _(p):
        length = points[lax.rem(owner[g * count + p], points.shape[0])]
        quarter = lax.div(length, 4)
        inverse = 1.0 / jnp.full((1, 128), length, jnp.int32).astype(jnp.float32)
        high, low = split(cosine(near + (deep % 2) * quarter, length, inverse))
        basis = jnp.concatenate([high, high, low, low][:copies], axis=0)
        inverse = jnp.concatenate([inverse] * (wide // 128), axis=1)
        turn = weight * cosine(far, length, inverse)
        cross = weight * cosine(far + (1 + 2 * (across % 2)) * quarter, length, inverse)
        start = pl.multiple_of(p * block, 8)
        own, other = coeffs[pl.ds(start, block), :], swapped[pl.ds(start, block), :]
        turned = jnp.concatenate(
            [own * turn[t : t + 1] + other * cross[t : t + 1] for t in range(tiles)], axis=0
        )
        head = turned.astype(jnp.bfloat16).astype(jnp.float32)
        parts = jnp.where(rest, turned - head, head).astype(jnp.bfloat16)
        values = dot(parts, basis)
        for t in range(tiles):
            kept = jnp.where(point + 128 * t < length, values[t * block : (t + 1) * block], 0.0)
            grid[p, :, :, 128 * t : 128 * (t + 1)] = kept.reshape(fields, level_total, 128)
        write(p).start()

    @pl.loop(0, count)
    def _(p):
        write(p).wait()


def body(groups, columns, spectra, legendre, wave_number, cycle_points, cycle_owner):
    fields, levels, waves, _, degrees = spectra.shape
    half = legendre.shape[2]
    count = 2 * half // groups
    lanes = count * SLOTS
    level_total = levels * groups
    segment = (RMAX + 128 * columns - 1) // (128 * columns) * 128
    vmem, smem = pl.BlockSpec(memory_space=pltpu.VMEM), pl.BlockSpec(memory_space=pltpu.SMEM)
    got = pl.pallas_call(
        functools.partial(spread, groups, columns),
        out_shape=jax.ShapeDtypeStruct((groups, columns, 4, lanes), jnp.float32),
        in_specs=[pl.BlockSpec(memory_space=pltpu.HBM)] * 2 + [smem, smem],
        out_specs=vmem,
        scratch_shapes=[
            pltpu.VMEM(spectra.shape, jnp.float32),
            pltpu.VMEM((waves, half, degrees), jnp.float32),
            pltpu.VMEM((waves, 16, degrees), jnp.float32),
            pltpu.VMEM((groups, 4, lanes), jnp.float32),
            pltpu.SemaphoreType.DMA((groups, columns)),
            pltpu.SemaphoreType.DMA((groups, columns)),
            pltpu.SemaphoreType.DMA((2,)),
        ],
        compiler_params=pltpu.CompilerParams(
            collective_id=0, has_side_effects=True, vmem_limit_bytes=VMEM_BYTES
        ),
        name="spread",
    )(spectra, jnp.swapaxes(legendre, 1, 2), wave_number, cycle_owner)
    wide = -(-3 * 4 * columns // 128) * 128
    block = fields * level_total
    return pl.pallas_call(
        functools.partial(synthesis, columns),
        out_shape=jax.ShapeDtypeStruct((count, fields, level_total, segment), jnp.float32),
        in_specs=[vmem, smem, smem, smem],
        out_specs=pl.BlockSpec(memory_space=pl.ANY),
        scratch_shapes=[
            pltpu.VMEM((count * block, wide), jnp.float32),
            pltpu.VMEM((count * block, wide), jnp.float32),
            pltpu.VMEM((count, fields, level_total, segment), jnp.float32),
            pltpu.SemaphoreType.DMA((count,)),
        ],
        compiler_params=pltpu.CompilerParams(vmem_limit_bytes=VMEM_BYTES),
        name="synthesis",
    )(got, wave_number, cycle_points, cycle_owner)


def solution(mesh):
    in_specs = (P(None, "grp", "wav", None, None), P("wav", None, None), P(), P(), P())
    out_specs = P("grp", None, None, "wav")
    groups, columns = mesh.shape["grp"], mesh.shape["wav"]
    return jax.shard_map(
        functools.partial(body, groups, columns),
        mesh=mesh,
        in_specs=in_specs,
        out_specs=out_specs,
        check_vma=False,
    )
```

profile of v0, /device:TPU:0, one launch (start us, length us, event | category | flops | bytes accessed | tf_op | source)
XLA Modules:
  0.0 16.7 jit_solution(17511350314316131260)
XLA Ops:
  0.0 12.9 %spread.1.got = f32[4,8,4,128]{3,2,1,0:T(4,128)} custom-call(f32[3,2,2,2,2560]{4,3,2,1,0:T(2,128)} %spec_in.1, f32[2,32,2560]{2,1,0:T(8,128)} %bitcast.1, s32[16]{0:T(128)} %wave.3, s32[64]{0:T(128)} %owner.3), custom_call_target="tpu_custom_call" | custom-call | tf_op jit(solution)/shard_map/spread/pallas_call | solution.py:214
  12.9 3.8 %synthesis.1 = f32[16,3,8,1408]{3,2,1,0:T(8,128)} custom-call(f32[4,8,4,128]{3,2,1,0:T(4,128)} %spread.1.got, s32[16]{0:T(128)} %wave.3, s32[32]{0:T(128)} %points.1, s32[64]{0:T(128)} %owner.3), custom_call_target="tpu_custom_call" | custom-call | tf_op jit(solution)/shard_map/synthesis/pallas_call | solution.py:235
where the time goes:
time: 16.9 us; the launch traced here: 16.7 us
  Pallas kernels  16.7 us (99%)
    pallas_call x1, Pallas kernels, body(): pl.pallas_call(functools.partial(spread, groups, columns), out_shape=jax....  12.9 us
    pallas_call x1, Pallas kernels, body(): pl.pallas_call(functools.partial(synthesis, columns), out_shape=jax.Shape...  3.8 us

commit v1 on v0

v1 whole, which is shorter than its diff:
```python
import functools
import math

import jax
import jax.numpy as jnp
from jax import lax
from jax.experimental import pallas as pl
from jax.experimental.pallas import tpu as pltpu
from jax.sharding import PartitionSpec as P

RMAX = 10256
SLOTS = 8
NEAR = 256
VMEM_BYTES = 24000 * 2**10
MESH = pl.DeviceIdType.MESH


def iota(shape, dim):
    return lax.broadcasted_iota(jnp.int32, shape, dim)


def split(x):
    high = x.astype(jnp.bfloat16)
    return high, (x - high.astype(jnp.float32)).astype(jnp.bfloat16)


def dot(a, b, dims=((1,), (0,))):
    return lax.dot_general(a, b, (dims, ((), ())), preferred_element_type=jnp.float32)


def one_hot(mask):
    return mask.astype(jnp.float32).astype(jnp.bfloat16)


def reduced(x, length, inverse):
    turns = jnp.floor(x.astype(jnp.float32) * inverse).astype(jnp.int32)
    left = x - turns * length
    left = jnp.where(left < 0, left + length, left)
    return jnp.where(left >= length, left - length, left)


def cosine(x, length, inverse):
    left = reduced(x, length, inverse)
    left = jnp.where(2 * left > length, left - length, left)
    half = left.astype(jnp.float32) * (inverse * math.pi)
    square = half * half
    series = jnp.full_like(square, 1.0 / math.factorial(13))
    for power in (11, 9, 7, 5, 3, 1):
        sign = -1.0 if power % 4 == 3 else 1.0
        series = series * square + sign / math.factorial(power)
    sine = series * half
    return 1.0 - 2.0 * sine * sine


def routing(owner, half, lanes):
    lane_row = iota((1, lanes), 1) // SLOTS
    cycle = jnp.zeros((1, lanes), jnp.int32)
    for row in range(2 * half):
        cycle = jnp.where(lane_row == row, owner[row], cycle)
    latitude = iota((half, lanes), 0)
    north, south = one_hot(latitude == cycle), one_hot(latitude + half == cycle)
    return jnp.concatenate([north, north, south, south], axis=0)


def tables(columns, count, segment, wide, wave, points, owner, basis, turn, cross, limit):
    depth = 4 * columns
    tile_rows = turn.shape[1]
    g, w = lax.axis_index("grp"), lax.axis_index("wav")
    half = points.shape[0]
    deep = iota((depth, NEAR), 0)
    deep_wave = jnp.zeros((depth, NEAR), jnp.int32)
    across = iota((tile_rows, wide), 1) % depth
    across_wave = jnp.zeros((tile_rows, wide), jnp.int32)
    for q in range(depth // 2):
        deep_wave = jnp.where(deep // 2 == q, wave[q], deep_wave)
        across_wave = jnp.where(across // 2 == q, wave[q], across_wave)
    near = deep_wave * iota((depth, NEAR), 1)
    far = across_wave * (w * segment + NEAR * iota((tile_rows, wide), 0))
    weight = jnp.where(across_wave == 0, 1.0, 2.0)
    point = iota((8, 128), 1) + w * segment

    @pl.loop(0, count, unroll=count if count <= 16 else 1)
    def _(p):
        length = points[lax.rem(owner[g * count + p], half)]
        quarter = lax.div(length, 4)
        inverse = 1.0 / jnp.full((1, 128), length, jnp.int32).astype(jnp.float32)
        across_near = jnp.concatenate([inverse] * (NEAR // 128), axis=1)
        high, low = split(cosine(near + (deep % 2) * quarter, length, across_near))
        basis[p, :depth] = high
        basis[p, depth:] = low
        inverse = jnp.concatenate([inverse] * (wide // 128), axis=1)
        turn[p] = weight * cosine(far, length, inverse)
        cross[p] = weight * cosine(far + (1 + 2 * (across % 2)) * quarter, length, inverse)
        limit[p] = length - point


def spread(groups, columns, segment, wide, *refs):
    spec_in, leg_in, wave_in, points_in, owner_in = refs[:5]
    out, basis, turn, cross, limit = refs[5:10]
    spec, leg, wave, points, owner, send, send_sem, recv_sem, load_sem = refs[10:]
    devices = groups * columns
    g, w = lax.axis_index("grp"), lax.axis_index("wav")
    me = w * groups + g
    waves, half, degrees = leg.shape
    lanes = send.shape[2]
    count = basis.shape[0]
    steps = degrees // 128
    fields, levels = spec_in.shape[:2]
    rows = 2 * fields * levels

    barrier = pltpu.get_barrier_semaphore()
    small = [
        pltpu.make_async_copy(wave_in, wave, load_sem.at[0]),
        pltpu.make_async_copy(points_in, points, load_sem.at[1]),
        pltpu.make_async_copy(owner_in, owner, load_sem.at[2]),
    ]
    large = [pltpu.make_async_copy(spec_in, spec, load_sem.at[3])]
    for q in range(waves):
        large.append(pltpu.make_async_copy(leg_in.at[q], leg.at[q], load_sem.at[4 + q]))
    for load in small + large:
        load.start()

    def each(act):
        @pl.loop(0, devices - 1, unroll=devices - 1 if devices <= 32 else 1)
        def _(i):
            to = i + (me <= i).astype(jnp.int32)
            act(lax.rem(to, groups), lax.div(to, groups))

    each(lambda *to: pl.semaphore_signal(barrier, inc=1, device_id=to, device_id_type=MESH))
    for load in small:
        load.wait()
    pick = routing(owner, half, groups * lanes)
    sign = jnp.where(iota((16, degrees), 1) % 2 == 0, 1.0, -1.0).astype(jnp.bfloat16)[:1]

    large[0].wait()
    parts = []
    for q in range(waves):
        number = wave[w * waves + q]
        inside = iota((16, degrees), 1) + jnp.where(iota((16, degrees), 0) < rows, number, degrees) < degrees
        high, low = split(jnp.where(inside, jnp.concatenate([spec[f, l, q] for f in range(fields) for l in range(levels)] + [jnp.zeros((16 - rows, degrees), jnp.float32)], axis=0), 0.0))
        large[1 + q].wait()
        table = jnp.concatenate(split(leg[q]), axis=0)
        table = jnp.concatenate([table, table * sign], axis=0)
        both = dot(jnp.concatenate([high, low], axis=0), table, ((1,), (1,)))
        parts.append(both[:16] + both[16:])
    fourier = jnp.concatenate(parts, axis=0)
    moved = dot(jnp.concatenate(split(fourier), axis=0), pick)
    height = fourier.shape[0]
    moved = moved[:height] + moved[height:]
    slot = iota((16, groups * lanes), 1) % SLOTS == iota((16, groups * lanes), 0) // 2
    message = jnp.zeros((8, groups * lanes), jnp.float32)
    for q in range(waves):
        kept = jnp.where(slot, moved[16 * q : 16 * q + 16], 0.0)
        kept = kept[:8] + kept[8:]
        kept = kept + pltpu.roll(kept, 4, 0)
        kept = kept + pltpu.roll(kept, 2, 0)
        message = jnp.where(iota(message.shape, 0) // 2 == q, kept, message)
    for to in range(groups):
        send[to] = message[:4, to * lanes : (to + 1) * lanes]
    out[g * columns + w] = send[g]

    pl.semaphore_wait(barrier, devices - 1)

    def start(to_g, to_w):
        pltpu.make_async_remote_copy(
            src_ref=send.at[to_g],
            dst_ref=out.at[g * columns + w],
            send_sem=send_sem,
            recv_sem=recv_sem,
            device_id=(to_g, to_w),
            device_id_type=MESH,
        ).start()

    each(start)
    tables(columns, count, segment, wide, wave, points, owner, basis, turn, cross, limit)
    others = out.at[pl.ds(0, devices - 1)]
    pltpu.make_async_copy(others, others, send_sem).wait()
    pltpu.make_async_copy(others, others, recv_sem).wait()


def swap(x):
    even = iota(x.shape, 0) % 2 == 0
    return jnp.where(even, pltpu.roll(x, x.shape[0] - 1, 0), pltpu.roll(x, 1, 0))


def by_field(groups, columns, fields, levels, got):
    depth, lanes = 4 * columns, got.shape[2]
    x = [got[i * columns : (i + 1) * columns].reshape(depth, lanes) for i in range(groups)]
    source = iota((depth, lanes), 1) % SLOTS // levels
    placed = []
    for f in range(fields):
        total = jnp.zeros((depth, lanes), jnp.float32)
        for i in range(groups):
            shift = (i - f) * levels % lanes
            total = jnp.where(source == i, pltpu.roll(x[i], shift, 1) if shift else x[i], total)
        placed.append(total)
    return placed


def arrange(groups, columns, copies, got, coeffs):
    fields, height, _ = coeffs.shape
    depth, lanes = 4 * columns, got.shape[2]
    count = lanes // SLOTS
    level_total = height // count
    levels = level_total // groups
    if level_total == SLOTS:
        same = one_hot(iota((lanes, lanes), 0) == iota((lanes, lanes), 1))
        same = jnp.concatenate([same, same], axis=1)
        for f, x in enumerate(by_field(groups, columns, fields, levels, got)):
            own, other = split(x), split(swap(x))
            source = [jnp.concatenate([own[h]] * copies + [other[h]] * copies, axis=0) for h in range(2)]
            coeffs[f] = dot(same, jnp.concatenate(source, axis=1), ((1,), (1,)))
        return
    x = [got[i * columns : (i + 1) * columns].reshape(depth, lanes) for i in range(groups)]
    x = jnp.concatenate(x, axis=1)
    own, other = split(x), split(swap(x))
    source = [jnp.concatenate([own[h]] * copies + [other[h]] * copies, axis=0) for h in range(2)]
    target = iota((height, 1), 0)
    level = lax.rem(target, level_total)
    for f in range(fields):
        at = (
            lax.div(level, levels) * lanes
            + lax.div(target, level_total) * SLOTS
            + f * levels
            + lax.rem(level, levels)
        )
        move = one_hot(iota((height, groups * lanes), 1) == at)
        coeffs[f] = dot(move, source[0], ((1,), (1,))) + dot(move, source[1], ((1,), (1,)))


def synthesis(groups, columns, got, basis, turn, cross, limit, out, coeffs, grid, out_sem):
    depth = 4 * columns
    count, fields, level_total, segment = grid.shape
    block = fields * level_total
    wide = turn.shape[2]
    copies = wide // depth
    tiles = -(-segment // NEAR)
    arrange(groups, columns, copies, got, coeffs)
    rest = (iota((block * tiles, wide), 1) // depth) % 2 == 1

    def write(p):
        return pltpu.make_async_copy(grid.at[p], out.at[p], out_sem.at[p])

    @pl.loop(0, count, unroll=16)
    def _(p):
        at = pl.ds(pl.multiple_of(p * level_total, 8), level_total)
        own = jnp.concatenate([coeffs[f, at, :wide] for f in range(fields)], axis=0)
        other = jnp.concatenate([coeffs[f, at, wide:] for f in range(fields)], axis=0)
        turns, crosses = turn[p], cross[p]
        turned = jnp.concatenate(
            [own * turns[t : t + 1] + other * crosses[t : t + 1] for t in range(tiles)], axis=0
        )
        head = turned.astype(jnp.bfloat16).astype(jnp.float32)
        parts = jnp.where(rest, turned - head, head).astype(jnp.bfloat16)
        high, low = basis[p, :depth], basis[p, depth:]
        values = dot(parts, jnp.concatenate([high, high, low, low][:copies], axis=0))
        room = limit[p]
        room = jnp.concatenate([room] * (level_total // 8), axis=0)
        for start in range(0, segment, 128):
            t, lane = start // NEAR, start % NEAR
            inside = room > start
            for f in range(fields):
                at = t * block + f * level_total
                kept = values[at : at + level_total, lane : lane + 128]
                grid[p, f, :, start : start + 128] = jnp.where(inside, kept, 0.0)
        write(p).start()

    @pl.loop(0, count)
    def _(p):
        write(p).wait()


def body(groups, columns, spectra, legendre, wave_number, cycle_points, cycle_owner):
    fields, levels, waves, parts, degrees = spectra.shape
    half = legendre.shape[2]
    count = 2 * half // groups
    lanes = count * SLOTS
    level_total = levels * groups
    depth = waves * 2 * columns
    segment = (RMAX + 128 * columns - 1) // (128 * columns) * 128
    wide = -(-3 * depth // 128) * 128
    tile_rows = -(-(-(-segment // NEAR)) // 8) * 8
    vmem, hbm = pl.BlockSpec(memory_space=pltpu.VMEM), pl.BlockSpec(memory_space=pltpu.HBM)
    inputs = (spectra, jnp.swapaxes(legendre, 1, 2), wave_number, cycle_points, cycle_owner)
    handed = pl.pallas_call(
        functools.partial(spread, groups, columns, segment, wide),
        out_shape=[
            pltpu.VMEM((groups * columns, 4, lanes), jnp.float32),
            pltpu.VMEM((count, 2 * depth, NEAR), jnp.bfloat16),
            pltpu.VMEM((count, tile_rows, wide), jnp.float32),
            pltpu.VMEM((count, tile_rows, wide), jnp.float32),
            pltpu.VMEM((count, 8, 128), jnp.int32),
        ],
        in_specs=[hbm] * 5,
        out_specs=[vmem] * 5,
        scratch_shapes=[
            pltpu.VMEM(spectra.shape, jnp.float32),
            pltpu.VMEM((waves, half, degrees), jnp.float32),
            pltpu.SMEM(wave_number.shape, jnp.int32),
            pltpu.SMEM(cycle_points.shape, jnp.int32),
            pltpu.SMEM(cycle_owner.shape, jnp.int32),
            pltpu.VMEM((groups, 4, lanes), jnp.float32),
            pltpu.SemaphoreType.DMA,
            pltpu.SemaphoreType.DMA,
            pltpu.SemaphoreType.DMA((4 + waves,)),
        ],
        compiler_params=pltpu.CompilerParams(
            collective_id=0, has_side_effects=True, vmem_limit_bytes=VMEM_BYTES
        ),
        name="spread",
    )(*[pltpu.with_memory_space_constraint(x, pltpu.HBM) for x in inputs])
    return pl.pallas_call(
        functools.partial(synthesis, groups, columns),
        out_shape=jax.ShapeDtypeStruct((count, fields, level_total, segment), jnp.float32),
        in_specs=[vmem] * 5,
        out_specs=pl.BlockSpec(memory_space=pl.ANY),
        scratch_shapes=[
            pltpu.VMEM((fields, count * level_total, 2 * wide), jnp.float32),
            pltpu.VMEM((count, fields, level_total, segment), jnp.float32),
            pltpu.SemaphoreType.DMA((count,)),
        ],
        compiler_params=pltpu.CompilerParams(vmem_limit_bytes=VMEM_BYTES),
        name="synthesis",
    )(*[pltpu.with_memory_space_constraint(x, pltpu.VMEM) for x in handed])


def solution(mesh):
    in_specs = (P(None, "grp", "wav", None, None), P("wav", None, None), P(), P(), P())
    out_specs = P("grp", None, None, "wav")
    groups, columns = mesh.shape["grp"], mesh.shape["wav"]
    return jax.shard_map(
        functools.partial(body, groups, columns),
        mesh=mesh,
        in_specs=in_specs,
        out_specs=out_specs,
        check_vma=False,
    )
```

time: 16.9 us -> 12.9 us (0.76)
  Pallas kernels: 16.7 us -> 12.8 us
    pallas_call x2, Pallas kernels: 16.7 us -> 12.8 us  [the longest x1 10.8 us: body(): pl.pallas_call(functools.partial(spread, groups, columns, segment, wide),...]
where the time goes in v1:
time: 12.9 us; the launch traced here: 12.8 us
  Pallas kernels  12.8 us (99%)
    pallas_call x1, Pallas kernels, body(): pl.pallas_call(functools.partial(spread, groups, columns, segment, wide),...  10.8 us
    pallas_call x1, Pallas kernels, body(): pl.pallas_call(functools.partial(synthesis, groups, columns), out_shape=j...  1.99 us

profile of v1, /device:TPU:0, one launch (start us, length us, event | category | flops | bytes accessed | tf_op | source)
XLA Modules:
  0.0 12.8 jit_solution(13684779793417514939)
XLA Ops:
  0.0 10.8 %spread.1 = (f32[32,4,128]{2,1,0:T(4,128)S(1)}, bf16[16,64,256]{2,1,0:T(8,128)(2,1)S(1)}, f32[16,8,128]{2,1,0:T(8,128)S(1)}, f32[16,8,128]{2,1,0:T(8,128)S(1)}, s32[16,8,128]{2,1,0:T(8,128)S(1)}) custom-call(f32[3,2,2,2,2560]{4,3,2,1,0:T(2,128)} %refs_0_.1, f32[2,32,2560]{2,1,0:T(8,128)} %bitcast.1, s32[16]{0:T(128)} %refs_2_.1, s32[32]{0:T(128)} %refs_3_.1, ...), custom_call_target="tpu_custom_call" | custom-call | tf_op jit(solution)/shard_map/spread/pallas_call | solution.py:285
  10.8 2.0 %synthesis.1 = f32[16,3,8,1408]{3,2,1,0:T(8,128)} custom-call(f32[32,4,128]{2,1,0:T(4,128)S(1)} %get-tuple-element.10.got, bf16[16,64,256]{2,1,0:T(8,128)(2,1)S(1)} %get-tuple-element.11.basis, f32[16,8,128]{2,1,0:T(8,128)S(1)} %get-tuple-element.12.turn, f32[16,8,128]{2,1,0:T(8,128)S(1)} %get-tuple-element.13.cross, s32[16,8,128]{2,1,0:T(8,128)S(1)} %get-tuple-element.14.limit), custom_call_target="tpu_custom_call" | custom-call | tf_op jit(solution)/shard_map/synthesis/pallas_call | solution.py:312

commit v2 on v1

--- a/solution.py
+++ b/solution.py
@@ -52,11 +52,16 @@
     return 1.0 - 2.0 * sine * sine
 
 
-def routing(owner, half, lanes):
-    lane_row = iota((1, lanes), 1) // SLOTS
-    cycle = jnp.zeros((1, lanes), jnp.int32)
-    for row in range(2 * half):
-        cycle = jnp.where(lane_row == row, owner[row], cycle)
+def routing(owner, half, groups, lanes):
+    count = 2 * half // groups
+    lane_row = iota((1, count * SLOTS), 1) // SLOTS
+    cycles = []
+    for to in range(groups):
+        cycle = jnp.zeros(lane_row.shape, jnp.int32)
+        for row in range(count):
+            cycle = jnp.where(lane_row == row, owner[to * count + row], cycle)
+        cycles.append(cycle)
+    cycle = jnp.concatenate(cycles, axis=1)
     latitude = iota((half, lanes), 0)
     north, south = one_hot(latitude == cycle), one_hot(latitude + half == cycle)
     return jnp.concatenate([north, north, south, south], axis=0)
@@ -129,19 +134,23 @@
     each(lambda *to: pl.semaphore_signal(barrier, inc=1, device_id=to, device_id_type=MESH))
     for load in small:
         load.wait()
-    pick = routing(owner, half, groups * lanes)
+    pick = routing(owner, half, groups, groups * lanes)
     sign = jnp.where(iota((16, degrees), 1) % 2 == 0, 1.0, -1.0).astype(jnp.bfloat16)[:1]
 
     large[0].wait()
-    parts = []
+    stacks = []
     for q in range(waves):
         number = wave[w * waves + q]
         inside = iota((16, degrees), 1) + jnp.where(iota((16, degrees), 0) < rows, number, degrees) < degrees
-        high, low = split(jnp.where(inside, jnp.concatenate([spec[f, l, q] for f in range(fields) for l in range(levels)] + [jnp.zeros((16 - rows, degrees), jnp.float32)], axis=0), 0.0))
-        large[1 + q].wait()
+        x = jnp.concatenate([spec[f, l, q] for f in range(fields) for l in range(levels)] + [jnp.zeros((16 - rows, degrees), jnp.float32)], axis=0)
+        stacks.append(jnp.concatenate(split(jnp.where(inside, x, 0.0)), axis=0))
+    for load in large[1:]:
+        load.wait()
+    parts = []
+    for q in range(waves):
         table = jnp.concatenate(split(leg[q]), axis=0)
         table = jnp.concatenate([table, table * sign], axis=0)
-        both = dot(jnp.concatenate([high, low], axis=0), table, ((1,), (1,)))
+        both = dot(stacks[q], table, ((1,), (1,)))
         parts.append(both[:16] + both[16:])
     fourier = jnp.concatenate(parts, axis=0)
     moved = dot(jnp.concatenate(split(fourier), axis=0), pick)

time: 12.9 us -> 12.6 us (0.977)
  Pallas kernels: 12.8 us -> 12.4 us
    pallas_call x1, Pallas kernels: 10.8 us -> 10.4 us  [body(): pl.pallas_call(functools.partial(spread, groups, columns, segment, wide),...]
where the time goes in v2:
time: 12.6 us; the launch traced here: 12.4 us
  Pallas kernels  12.4 us (98%)
    pallas_call x1, Pallas kernels, body(): pl.pallas_call(functools.partial(spread, groups, columns, segment, wide),...  10.4 us
    pallas_call x1, Pallas kernels, body(): pl.pallas_call(functools.partial(synthesis, groups, columns), out_shape=j...  1.99 us

profile of v2, /device:TPU:0, one launch (start us, length us, event | category | flops | bytes accessed | tf_op | source)
XLA Modules:
  0.0 12.4 jit_solution(2602332034341885698)
XLA Ops:
  0.0 10.4 %spread.1 = (f32[32,4,128]{2,1,0:T(4,128)S(1)}, bf16[16,64,256]{2,1,0:T(8,128)(2,1)S(1)}, f32[16,8,128]{2,1,0:T(8,128)S(1)}, f32[16,8,128]{2,1,0:T(8,128)S(1)}, s32[16,8,128]{2,1,0:T(8,128)S(1)}) custom-call(f32[3,2,2,2,2560]{4,3,2,1,0:T(2,128)} %refs_0_.1, f32[2,32,2560]{2,1,0:T(8,128)} %bitcast.1, s32[16]{0:T(128)} %refs_2_.1, s32[32]{0:T(128)} %refs_3_.1, ...), custom_call_target="tpu_custom_call" | custom-call | tf_op jit(solution)/shard_map/spread/pallas_call | solution.py:294
  10.4 2.0 %synthesis.1 = f32[16,3,8,1408]{3,2,1,0:T(8,128)} custom-call(f32[32,4,128]{2,1,0:T(4,128)S(1)} %get-tuple-element.10.got, bf16[16,64,256]{2,1,0:T(8,128)(2,1)S(1)} %get-tuple-element.11.basis, f32[16,8,128]{2,1,0:T(8,128)S(1)} %get-tuple-element.12.turn, f32[16,8,128]{2,1,0:T(8,128)S(1)} %get-tuple-element.13.cross, s32[16,8,128]{2,1,0:T(8,128)S(1)} %get-tuple-element.14.limit), custom_call_target="tpu_custom_call" | custom-call | tf_op jit(solution)/shard_map/synthesis/pallas_call | solution.py:321

commit v3 on v2

--- a/solution.py
+++ b/solution.py
@@ -120,8 +120,7 @@
         pltpu.make_async_copy(owner_in, owner, load_sem.at[2]),
     ]
     large = [pltpu.make_async_copy(spec_in, spec, load_sem.at[3])]
-    for q in range(waves):
-        large.append(pltpu.make_async_copy(leg_in.at[q], leg.at[q], load_sem.at[4 + q]))
+    large.append(pltpu.make_async_copy(leg_in, leg, load_sem.at[4]))
     for load in small + large:
         load.start()
 
@@ -135,24 +134,40 @@
     for load in small:
         load.wait()
     pick = routing(owner, half, groups, groups * lanes)
-    sign = jnp.where(iota((16, degrees), 1) % 2 == 0, 1.0, -1.0).astype(jnp.bfloat16)[:1]
-
+    sign = jnp.where(iota((16, 128), 1) % 2 == 0, 1.0, -1.0).astype(jnp.bfloat16)[:1]
     large[0].wait()
-    stacks = []
-    for q in range(waves):
+    halves = []
+    for q in range(2):
         number = wave[w * waves + q]
         inside = iota((16, degrees), 1) + jnp.where(iota((16, degrees), 0) < rows, number, degrees) < degrees
-        x = jnp.concatenate([spec[f, l, q] for f in range(fields) for l in range(levels)] + [jnp.zeros((16 - rows, degrees), jnp.float32)], axis=0)
-        stacks.append(jnp.concatenate(split(jnp.where(inside, x, 0.0)), axis=0))
+        x = [spec[f, l, q] for f in range(fields) for l in range(levels)]
+        x = jnp.concatenate(x + [jnp.zeros((16 - rows, degrees), jnp.float32)], axis=0)
+        halves.append(split(jnp.where(inside, x, 0.0)))
+
+    def tile(x, k):
+        if 0 <= k < steps:
+            return x[:, 128 * k : 128 * (k + 1)]
+        return jnp.zeros((x.shape[0], 128), x.dtype)
+
+    tall = [
+        jnp.concatenate(
+            [tile(halves[q][h], steps - i if q else i) for h in range(2) for q in range(2)], axis=0
+        )
+        for i in range(steps + 1)
+    ]
     for load in large[1:]:
         load.wait()
-    parts = []
-    for q in range(waves):
-        table = jnp.concatenate(split(leg[q]), axis=0)
-        table = jnp.concatenate([table, table * sign], axis=0)
-        both = dot(stacks[q], table, ((1,), (1,)))
-        parts.append(both[:16] + both[16:])
-    fourier = jnp.concatenate(parts, axis=0)
+    first = jnp.full((half, 128), wave[w * waves], jnp.int32)
+    table = []
+    for i in range(steps + 1):
+        piece = leg[0 if i < steps else 1, :, pl.ds(128 * i if i < steps else 0, 128)]
+        if 0 < i < steps:
+            other = leg[1, :, pl.ds(128 * (steps - i), 128)]
+            piece = jnp.where(first + 128 * i < degrees, piece, other)
+        piece = jnp.concatenate(split(piece), axis=0)
+        table.append(jnp.concatenate([piece, piece * sign], axis=0))
+    fourier = dot(jnp.concatenate(tall, axis=1), jnp.concatenate(table, axis=1), ((1,), (1,)))
+    fourier = fourier[:32] + fourier[32:]
     moved = dot(jnp.concatenate(split(fourier), axis=0), pick)
     height = fourier.shape[0]
     moved = moved[:height] + moved[height:]
@@ -248,7 +263,7 @@
     rest = (iota((block * tiles, wide), 1) // depth) % 2 == 1
 
     def write(p):
-        return pltpu.make_async_copy(grid.at[p], out.at[p], out_sem.at[p])
+        return pltpu.make_async_copy(grid.at[p], out.at[p], out_sem)
 
     @pl.loop(0, count, unroll=16)
     def _(p):
@@ -274,9 +289,7 @@
                 grid[p, f, :, start : start + 128] = jnp.where(inside, kept, 0.0)
         write(p).start()
 
-    @pl.loop(0, count)
-    def _(p):
-        write(p).wait()
+    pltpu.make_async_copy(grid, out, out_sem).wait()
 
 
 def body(groups, columns, spectra, legendre, wave_number, cycle_points, cycle_owner):
@@ -311,7 +324,7 @@
             pltpu.VMEM((groups, 4, lanes), jnp.float32),
             pltpu.SemaphoreType.DMA,
             pltpu.SemaphoreType.DMA,
-            pltpu.SemaphoreType.DMA((4 + waves,)),
+            pltpu.SemaphoreType.DMA((5,)),
         ],
         compiler_params=pltpu.CompilerParams(
             collective_id=0, has_side_effects=True, vmem_limit_bytes=VMEM_BYTES
@@ -326,7 +339,7 @@
         scratch_shapes=[
             pltpu.VMEM((fields, count * level_total, 2 * wide), jnp.float32),
             pltpu.VMEM((count, fields, level_total, segment), jnp.float32),
-            pltpu.SemaphoreType.DMA((count,)),
+            pltpu.SemaphoreType.DMA,
         ],
         compiler_params=pltpu.CompilerParams(vmem_limit_bytes=VMEM_BYTES),
         name="synthesis",

time: 12.6 us -> 12.3 us (0.976)
  Pallas kernels: 12.4 us -> 12.2 us
    pallas_call x1, Pallas kernels: 1.99 us -> 1.86 us  [body(): pl.pallas_call(functools.partial(synthesis, groups, columns), out_shape=j...]
where the time goes in v3:
time: 12.3 us; the launch traced here: 12.2 us
  Pallas kernels  12.2 us (99%)
    pallas_call x1, Pallas kernels, body(): pl.pallas_call(functools.partial(spread, groups, columns, segment, wide),...  10.3 us
    pallas_call x1, Pallas kernels, body(): pl.pallas_call(functools.partial(synthesis, groups, columns), out_shape=j...  1.86 us

profile of v3, /device:TPU:0, one launch (start us, length us, event | category | flops | bytes accessed | tf_op | source)
XLA Modules:
  0.0 12.2 jit_solution(17535364975075715953)
XLA Ops:
  0.0 10.3 %spread.1 = (f32[32,4,128]{2,1,0:T(4,128)S(1)}, bf16[16,64,256]{2,1,0:T(8,128)(2,1)S(1)}, f32[16,8,128]{2,1,0:T(8,128)S(1)}, f32[16,8,128]{2,1,0:T(8,128)S(1)}, s32[16,8,128]{2,1,0:T(8,128)S(1)}) custom-call(f32[3,2,2,2,2560]{4,3,2,1,0:T(2,128)} %refs_0_.1, f32[2,32,2560]{2,1,0:T(8,128)} %bitcast.1, s32[16]{0:T(128)} %refs_2_.1, s32[32]{0:T(128)} %refs_3_.1, ...), custom_call_target="tpu_custom_call" | custom-call | tf_op jit(solution)/shard_map/spread/pallas_call | solution.py:307
  10.3 1.9 %synthesis.1 = f32[16,3,8,1408]{3,2,1,0:T(8,128)} custom-call(f32[32,4,128]{2,1,0:T(4,128)S(1)} %get-tuple-element.10.got, bf16[16,64,256]{2,1,0:T(8,128)(2,1)S(1)} %get-tuple-element.11.basis, f32[16,8,128]{2,1,0:T(8,128)S(1)} %get-tuple-element.12.turn, f32[16,8,128]{2,1,0:T(8,128)S(1)} %get-tuple-element.13.cross, s32[16,8,128]{2,1,0:T(8,128)S(1)} %get-tuple-element.14.limit), custom_call_target="tpu_custom_call" | custom-call | tf_op jit(solution)/shard_map/synthesis/pallas_call | solution.py:334

commit v4 on v3

--- a/solution.py
+++ b/solution.py
@@ -171,7 +171,8 @@
     moved = dot(jnp.concatenate(split(fourier), axis=0), pick)
     height = fourier.shape[0]
     moved = moved[:height] + moved[height:]
-    slot = iota((16, groups * lanes), 1) % SLOTS == iota((16, groups * lanes), 0) // 2
+    turned = (groups - g) * levels if groups * levels == SLOTS else 0
+    slot = (iota((16, groups * lanes), 1) + turned) % SLOTS == iota((16, groups * lanes), 0) // 2
     message = jnp.zeros((8, groups * lanes), jnp.float32)
     for q in range(waves):
         kept = jnp.where(slot, moved[16 * q : 16 * q + 16], 0.0)
@@ -213,10 +214,9 @@
     source = iota((depth, lanes), 1) % SLOTS // levels
     placed = []
     for f in range(fields):
-        total = jnp.zeros((depth, lanes), jnp.float32)
-        for i in range(groups):
-            shift = (i - f) * levels % lanes
-            total = jnp.where(source == i, pltpu.roll(x[i], shift, 1) if shift else x[i], total)
+        total = x[0]
+        for i in range(1, groups):
+            total = jnp.where(source == (i + f) % groups, x[i], total)
         placed.append(total)
     return placed
 
@@ -228,12 +228,9 @@
     level_total = height // count
     levels = level_total // groups
     if level_total == SLOTS:
-        same = one_hot(iota((lanes, lanes), 0) == iota((lanes, lanes), 1))
-        same = jnp.concatenate([same, same], axis=1)
         for f, x in enumerate(by_field(groups, columns, fields, levels, got)):
-            own, other = split(x), split(swap(x))
-            source = [jnp.concatenate([own[h]] * copies + [other[h]] * copies, axis=0) for h in range(2)]
-            coeffs[f] = dot(same, jnp.concatenate(source, axis=1), ((1,), (1,)))
+            coeffs[f, :, : copies * depth] = jnp.concatenate([x] * copies, axis=0).T
+            coeffs[f, :, copies * depth :] = jnp.concatenate([swap(x)] * copies, axis=0).T
         return
     x = [got[i * columns : (i + 1) * columns].reshape(depth, lanes) for i in range(groups)]
     x = jnp.concatenate(x, axis=1)
@@ -268,8 +265,14 @@
     @pl.loop(0, count, unroll=16)
     def _(p):
         at = pl.ds(pl.multiple_of(p * level_total, 8), level_total)
-        own = jnp.concatenate([coeffs[f, at, :wide] for f in range(fields)], axis=0)
-        other = jnp.concatenate([coeffs[f, at, wide:] for f in range(fields)], axis=0)
+        own, other = [], []
+        for f in range(fields):
+            x = coeffs[f, at, :]
+            if level_total == SLOTS and f:
+                x = pltpu.roll(x, SLOTS - f * level_total // groups, 0)
+            own.append(x[:, :wide])
+            other.append(x[:, wide:])
+        own, other = jnp.concatenate(own, axis=0), jnp.concatenate(other, axis=0)
         turns, crosses = turn[p], cross[p]
         turned = jnp.concatenate(
             [own * turns[t : t + 1] + other * crosses[t : t + 1] for t in range(tiles)], axis=0

time: 12.3 us -> 12.1 us (0.984)
  Pallas kernels: 12.2 us -> 12 us
    pallas_call x1, Pallas kernels: 1.86 us -> 1.66 us  [body(): pl.pallas_call(functools.partial(synthesis, groups, columns), out_shape=j...]
where the time goes in v4:
time: 12.1 us; the launch traced here: 12 us
  Pallas kernels  12 us (99%)
    pallas_call x1, Pallas kernels, body(): pl.pallas_call(functools.partial(spread, groups, columns, segment, wide),...  10.3 us
    pallas_call x1, Pallas kernels, body(): pl.pallas_call(functools.partial(synthesis, groups, columns), out_shape=j...  1.66 us

profile of v4, /device:TPU:0, one launch (start us, length us, event | category | flops | bytes accessed | tf_op | source)
XLA Modules:
  0.0 12.0 jit_solution(13509763745176979045)
XLA Ops:
  0.0 10.3 %spread.1 = (f32[32,4,128]{2,1,0:T(4,128)S(1)}, bf16[16,64,256]{2,1,0:T(8,128)(2,1)S(1)}, f32[16,8,128]{2,1,0:T(8,128)S(1)}, f32[16,8,128]{2,1,0:T(8,128)S(1)}, s32[16,8,128]{2,1,0:T(8,128)S(1)}) custom-call(f32[3,2,2,2,2560]{4,3,2,1,0:T(2,128)} %refs_0_.1, f32[2,32,2560]{2,1,0:T(8,128)} %bitcast.1, s32[16]{0:T(128)} %refs_2_.1, s32[32]{0:T(128)} %refs_3_.1, ...), custom_call_target="tpu_custom_call" | custom-call | tf_op jit(solution)/shard_map/spread/pallas_call | solution.py:310
  10.3 1.7 %synthesis.1 = f32[16,3,8,1408]{3,2,1,0:T(8,128)} custom-call(f32[32,4,128]{2,1,0:T(4,128)S(1)} %get-tuple-element.10.got, bf16[16,64,256]{2,1,0:T(8,128)(2,1)S(1)} %get-tuple-element.11.basis, f32[16,8,128]{2,1,0:T(8,128)S(1)} %get-tuple-element.12.turn, f32[16,8,128]{2,1,0:T(8,128)S(1)} %get-tuple-element.13.cross, s32[16,8,128]{2,1,0:T(8,128)S(1)} %get-tuple-element.14.limit), custom_call_target="tpu_custom_call" | custom-call | tf_op jit(solution)/shard_map/synthesis/pallas_call | solution.py:337

commit v5 on v4

--- a/solution.py
+++ b/solution.py
@@ -131,9 +131,7 @@
             act(lax.rem(to, groups), lax.div(to, groups))
 
     each(lambda *to: pl.semaphore_signal(barrier, inc=1, device_id=to, device_id_type=MESH))
-    for load in small:
-        load.wait()
-    pick = routing(owner, half, groups, groups * lanes)
+    small[0].wait()
     sign = jnp.where(iota((16, 128), 1) % 2 == 0, 1.0, -1.0).astype(jnp.bfloat16)[:1]
     large[0].wait()
     halves = []
@@ -155,8 +153,9 @@
         )
         for i in range(steps + 1)
     ]
-    for load in large[1:]:
+    for load in large[1:] + small[1:]:
         load.wait()
+    pick = routing(owner, half, groups, groups * lanes)
     first = jnp.full((half, 128), wave[w * waves], jnp.int32)
     table = []
     for i in range(steps + 1):
@@ -182,7 +181,6 @@
         message = jnp.where(iota(message.shape, 0) // 2 == q, kept, message)
     for to in range(groups):
         send[to] = message[:4, to * lanes : (to + 1) * lanes]
-    out[g * columns + w] = send[g]
 
     pl.semaphore_wait(barrier, devices - 1)
 
@@ -197,6 +195,7 @@
         ).start()
 
     each(start)
+    out[g * columns + w] = send[g]
     tables(columns, count, segment, wide, wave, points, owner, basis, turn, cross, limit)
     others = out.at[pl.ds(0, devices - 1)]
     pltpu.make_async_copy(others, others, send_sem).wait()

time: 12.1 us -> 12.2 us (level)
  no operation moved by 1% of the time
where the time goes in v5:
time: 12.2 us; the launch traced here: 12 us
  Pallas kernels  12 us (98%)
    pallas_call x1, Pallas kernels, body(): pl.pallas_call(functools.partial(spread, groups, columns, segment, wide),...  10.3 us
    pallas_call x1, Pallas kernels, body(): pl.pallas_call(functools.partial(synthesis, groups, columns), out_shape=j...  1.66 us

profile of v5, /device:TPU:0, one launch (start us, length us, event | category | flops | bytes accessed | tf_op | source)
XLA Modules:
  0.0 12.0 jit_solution(4595733412076183445)
XLA Ops:
  0.0 10.3 %spread.1 = (f32[32,4,128]{2,1,0:T(4,128)S(1)}, bf16[16,64,256]{2,1,0:T(8,128)(2,1)S(1)}, f32[16,8,128]{2,1,0:T(8,128)S(1)}, f32[16,8,128]{2,1,0:T(8,128)S(1)}, s32[16,8,128]{2,1,0:T(8,128)S(1)}) custom-call(f32[3,2,2,2,2560]{4,3,2,1,0:T(2,128)} %refs_0_.1, f32[2,32,2560]{2,1,0:T(8,128)} %bitcast.1, s32[16]{0:T(128)} %refs_2_.1, s32[32]{0:T(128)} %refs_3_.1, ...), custom_call_target="tpu_custom_call" | custom-call | tf_op jit(solution)/shard_map/spread/pallas_call | solution.py:309
  10.4 1.7 %synthesis.1 = f32[16,3,8,1408]{3,2,1,0:T(8,128)} custom-call(f32[32,4,128]{2,1,0:T(4,128)S(1)} %get-tuple-element.10.got, bf16[16,64,256]{2,1,0:T(8,128)(2,1)S(1)} %get-tuple-element.11.basis, f32[16,8,128]{2,1,0:T(8,128)S(1)} %get-tuple-element.12.turn, f32[16,8,128]{2,1,0:T(8,128)S(1)} %get-tuple-element.13.cross, s32[16,8,128]{2,1,0:T(8,128)S(1)} %get-tuple-element.14.limit), custom_call_target="tpu_custom_call" | custom-call | tf_op jit(solution)/shard_map/synthesis/pallas_call | solution.py:336

commit v6 on v5

--- a/solution.py
+++ b/solution.py
@@ -121,8 +121,12 @@
     ]
     large = [pltpu.make_async_copy(spec_in, spec, load_sem.at[3])]
     large.append(pltpu.make_async_copy(leg_in, leg, load_sem.at[4]))
-    for load in small + large:
+    for load in small:
         load.start()
+    for f in range(spec_in.shape[0]):
+        for l in range(spec_in.shape[1]):
+            pltpu.make_async_copy(spec_in.at[f, l], spec.at[f, l], load_sem.at[3]).start()
+    large[1].start()
 
     def each(act):
         @pl.loop(0, devices - 1, unroll=devices - 1 if devices <= 32 else 1)

time: 12.2 us -> 12.2 us (level)
  no operation moved by 1% of the time
where the time goes in v6:
time: 12.2 us; the launch traced here: 12 us
  Pallas kernels  12 us (98%)
    pallas_call x1, Pallas kernels, body(): pl.pallas_call(functools.partial(spread, groups, columns, segment, wide),...  10.4 us
    pallas_call x1, Pallas kernels, body(): pl.pallas_call(functools.partial(synthesis, groups, columns), out_shape=j...  1.66 us

profile of v6, /device:TPU:0, one launch (start us, length us, event | category | flops | bytes accessed | tf_op | source)
XLA Modules:
  0.0 12.0 jit_solution(193417038427390377)
XLA Ops:
  0.0 10.4 %spread.1 = (f32[32,4,128]{2,1,0:T(4,128)S(1)}, bf16[16,64,256]{2,1,0:T(8,128)(2,1)S(1)}, f32[16,8,128]{2,1,0:T(8,128)S(1)}, f32[16,8,128]{2,1,0:T(8,128)S(1)}, s32[16,8,128]{2,1,0:T(8,128)S(1)}) custom-call(f32[3,2,2,2,2560]{4,3,2,1,0:T(2,128)} %refs_0_.1, f32[2,32,2560]{2,1,0:T(8,128)} %bitcast.1, s32[16]{0:T(128)} %refs_2_.1, s32[32]{0:T(128)} %refs_3_.1, ...), custom_call_target="tpu_custom_call" | custom-call | tf_op jit(solution)/shard_map/spread/pallas_call | solution.py:313
  10.4 1.7 %synthesis.1 = f32[16,3,8,1408]{3,2,1,0:T(8,128)} custom-call(f32[32,4,128]{2,1,0:T(4,128)S(1)} %get-tuple-element.10.got, bf16[16,64,256]{2,1,0:T(8,128)(2,1)S(1)} %get-tuple-element.11.basis, f32[16,8,128]{2,1,0:T(8,128)S(1)} %get-tuple-element.12.turn, f32[16,8,128]{2,1,0:T(8,128)S(1)} %get-tuple-element.13.cross, s32[16,8,128]{2,1,0:T(8,128)S(1)} %get-tuple-element.14.limit), custom_call_target="tpu_custom_call" | custom-call | tf_op jit(solution)/shard_map/synthesis/pallas_call | solution.py:340
